TPU v7x, 32 devices: a whole 2x2x4 slice. The times are simulated.
32 devices in a mesh: groups: 2 (over x), expert: 16 (over z, y, core).
Axes of the slice: x: 2, y: 2, z: 4, core: 2. Of those that a mesh axis runs over, the one named last changes fastest.
Arguments:
- tokens: bfloat16 [4096, 4096], P(('groups', 'expert')), parts along dimension 0, may hold values from -6 to 6
- routing: int32 [4096], P(('groups', 'expert')), parts along dimension 0, may hold values from 0 to 7, as said below
- capacity_slot: int32 [4096], P(('groups', 'expert')), parts along dimension 0, may hold values from 0 to 24, as said below
- router_prob: float32 [4096], P(('groups', 'expert')), parts along dimension 0, may hold values from 0.3 to 1
- norm_gain: float32 [4096], replicated, may hold values from 0.5 to 2
- expert_in: bfloat16 [16, 4096, 2560], P('expert'), may hold values from -0.09375 to 0.09375
- expert_out: bfloat16 [16, 2560, 4096], P('expert'), may hold values from -0.078125 to 0.078125
Outputs:
- layer_output: bfloat16 [4096, 4096], P(('groups', 'expert')), parts along dimension 0
There are 2 independent parts, one for each index of `groups`. A program takes and returns all parts, laid end to end along the dimension named above; an argument that names none is the same for every part. Nothing has to cross between parts.
Inputs may be any that keep to these rules, and one draw needn't show every extreme that they name: `routing`: on the rows of one device one expert, the same on every device of a part, is named by exactly 25 rows; every other expert by at most 20 rows. `capacity_slot`: on the rows of one device the rows that name one expert have distinct slots; those of the expert named by 20 + 5 rows take every slot below 25, all others stay below 20.
All inputs are finite; a program needn't handle non-finite values.
Results may differ from a plain program's by a relative error of at most 0.0048.
Values may be sent and summed in bfloat16 or wider, within the bound.
A program may use at most 128 MiB of HBM per device.

v0:
```python
import jax
import jax.numpy as jnp
from jax import lax
from jax.sharding import PartitionSpec as P

EXP_WIN = 8
CAP = 20


def from_partner(x, axis, distance):
    return lax.ppermute(x, axis, [(i, i ^ 1 << distance) for i in range(lax.axis_size(axis))])


def per_device(tokens, routing, capacity_slot, router_prob, norm_gain, expert_in, expert_out):
    devices = lax.axis_size("expert")
    holders = devices // EXP_WIN
    features = tokens.shape[1]
    slots_total = EXP_WIN * CAP
    widened = tokens.astype(jnp.float32)
    normed = (
        widened * lax.rsqrt(jnp.mean(widened * widened, axis=-1, keepdims=True) + 1e-06) * norm_gain
    ).astype(jnp.bfloat16)
    kept_rows = capacity_slot < CAP
    target = jnp.where(kept_rows, routing * CAP + capacity_slot, -1)
    placing = (target[None, :] == jnp.arange(slots_total, dtype=jnp.int32)[:, None]).astype(
        jnp.bfloat16
    )
    buckets = (
        jnp.dot(placing, normed, preferred_element_type=jnp.float32)
        .astype(jnp.bfloat16)
        .reshape(EXP_WIN, CAP, features)
    )
    weight_in = expert_in[0]
    weight_out = expert_out[0]
    slice_width = features // holders
    sliced = (
        buckets.reshape(EXP_WIN, CAP, holders, slice_width)
        .transpose(0, 2, 1, 3)
        .reshape(devices, CAP, slice_width)
    )
    bucket_rows = lax.all_to_all(sliced, "expert", split_axis=0, concat_axis=0, tiled=True)
    lowest = lax.axis_index("expert")
    for bit_pos in range(holders.bit_length() - 1):
        partner = from_partner(bucket_rows, "expert", bit_pos)
        upper_half = lowest >> bit_pos & 1 == 1
        bucket_rows = jnp.where(
            upper_half,
            jnp.concatenate([partner, bucket_rows], 2),
            jnp.concatenate([bucket_rows, partner], 2),
        )
    slot_count = bucket_rows.shape[1]
    flat_rows = bucket_rows.reshape(devices * slot_count, features)
    hidden = jnp.maximum(
        jnp.dot(flat_rows, weight_in, preferred_element_type=jnp.float32), 0.0
    ).astype(jnp.bfloat16)
    partial_value = jnp.dot(hidden, weight_out, preferred_element_type=jnp.float32).astype(
        jnp.bfloat16
    )
    partial_value = partial_value.reshape(devices, slot_count, features)
    returned = lax.all_to_all(partial_value, "expert", split_axis=0, concat_axis=0, tiled=True)
    combined = (
        returned.reshape(EXP_WIN, holders, CAP, features)
        .astype(jnp.float32)
        .sum(axis=1)
        .reshape(slots_total, features)
    )
    picked = jnp.take(combined, jnp.clip(target, 0, slots_total - 1), axis=0)
    branch = jnp.where(kept_rows[:, None], picked, 0.0)
    return (widened + router_prob[:, None] * branch).astype(jnp.bfloat16)


def solution(mesh):
    placed = (
        P(("groups", "expert"), None),
        P(("groups", "expert")),
        P(("groups", "expert")),
        P(("groups", "expert")),
        P(),
        P("expert", None, None),
        P("expert", None, None),
    )
    return jax.shard_map(
        per_device,
        mesh=mesh,
        in_specs=placed,
        out_specs=P(("groups", "expert"), None),
        check_vma=False,
    )
```

profile of v0, /device:TPU:15, one launch (start us, length us, event | category | flops | bytes accessed | tf_op | source)
XLA Modules:
  0.0 171.0 jit_solution(3244730296376877706)
XLA Ops:
  0.0 1.5 fusion.27
  1.5 0.7 compare_and_fusion
  2.2 1.8 %convolution_convert_fusion = bf16[160,4096]{1,0:T(8,128)(2,1)S(1)} fusion(bf16[128,4096]{1,0:T(8,128)(2,1)} %param.7, f32[4096]{0:T(1024)} %param.11, f32[128]{0:T(128)S(1)} %add_rsqrt_fusion, s32[128]{0:T(128)S(1)} %get-tuple-element.7), kind=kOutput, calls=%fused_computation.7 | convolution fusion | flops 170545152 | bytes 2376704 | tf_op jit(solution)/shard_map/dot_general | solution.py:29
  4.0 1.0 reshape_reshape.3
  5.0 0.6 copy.17
  5.6 42.4 %all_to_all.10 = bf16[16,20,2048]{2,1,0:T(8,128)(2,1)S(1)} all-to-all(bf16[16,20,2048]{2,1,0:T(8,128)(2,1)S(1)} %bitcast.20), channel_id=1, replica_groups=mesh['groups'=2,'expert'=16] {'expert'}, dimensions={0} | all-to-all | bytes 2621440 | tf_op jit(solution)/shard_map/all_to_all | solution.py:41
  48.1 1.8 %copy.15 = bf16[16,20,2048]{2,0,1:T(8,128)(2,1)} copy(bf16[16,20,2048]{2,1,0:T(8,128)(2,1)S(1)} %all_to_all.10) | data formatting | bytes 2621440 | tf_op jit(solution)/shard_map/all_to_all | solution.py:41
  49.9 0.2 collective-permute-start
  50.1 1.2 concatenate.13
  51.3 1.8 %collective-permute-done = bf16[16,20,2048]{2,0,1:T(8,128)(2,1)S(1)} collective-permute-done((bf16[16,20,2048]{2,0,1:T(8,128)(2,1)}, bf16[16,20,2048]{2,0,1:T(8,128)(2,1)S(1)}, u32[]{:S(2)}, u32[]{:S(2)}) %collective-permute-start) | collective-permute-done | bytes 1310752 | tf_op jit(solution)/shard_map/ppermute | solution.py:11
  53.1 0.7 copy.16
  53.8 1.2 concatenate.12
  55.1 28.3 %fusion.4 = bf16[320,4096]{1,0:T(8,128)(2,1)S(1)} fusion(bf16[1,2560,4096]{2,1,0:T(8,128)(2,1)} %param.13, bf16[1,4096,2560]{2,1,0:T(8,128)(2,1)} %param.12, bf16[320,2048]{1,0:T(8,128)(2,1)} %concatenate.13, bf16[320,2048]{1,0:T(8,128)(2,1)} %concatenate.12, pred[]{:T(512)S(6)} %eq.16), kind=kOutput, calls=%fused_computation.6 | convolution fusion | flops 13436518400 | bytes 47185920 | tf_op jit(solution)/shard_map/dot_general | solution.py:56
  83.4 2.4 %reshape.35 = bf16[16,20,4096]{2,1,0:T(8,128)(2,1)} reshape(bf16[320,4096]{1,0:T(8,128)(2,1)S(1)} %fusion.4) | data formatting | bytes 5242880 | tf_op jit(solution)/shard_map/reshape | solution.py:59
  85.7 5.0 %all-to-all-start.1 = ((bf16[16,20,4096]{2,1,0:T(8,128)(2,1)}), bf16[16,20,4096]{2,1,0:T(8,128)(2,1)S(1)}, u32[]{:S(2)}, u32[]{:S(2)}) async-start(bf16[16,20,4096]{2,1,0:T(8,128)(2,1)} %reshape.35), calls=%async_computation.1 | async-start | bytes 6291456 | tf_op jit(solution)/shard_map/all_to_all | solution.py:60
  90.8 69.9 %all-to-all-done.1 = bf16[16,20,4096]{2,1,0:T(8,128)(2,1)S(1)} async-done(((bf16[16,20,4096]{2,1,0:T(8,128)(2,1)}), bf16[16,20,4096]{2,1,0:T(8,128)(2,1)S(1)}, u32[]{:S(2)}, u32[]{:S(2)}) %all-to-all-start.1) | async-done | bytes 2621472 | tf_op jit(solution)/shard_map/all_to_all | solution.py:60
  160.6 2.3 %convert_reduce_fusion = f32[8,20,4096]{2,1,0:T(8,128)} fusion(bf16[16,20,4096]{2,1,0:T(8,128)(2,1)S(1)} %all-to-all-done.1), kind=kLoop, calls=%fused_computation.5 | loop fusion | flops 1966080 | bytes 5242880 | tf_op jit(solution)/shard_map/reduce_sum | solution.py:64
  163.0 2.0 %reshape.36 = f32[160,4096]{1,0:T(8,128)S(1)} reshape(f32[8,20,4096]{2,1,0:T(8,128)} %convert_reduce_fusion) | data formatting | bytes 5242880 | tf_op jit(solution)/shard_map/reshape | solution.py:65
  165.0 0.0 copy-start
  165.0 2.6 %gather_fusion = f32[128,4096]{1,0:T(8,128)} fusion(f32[160,4096]{1,0:T(8,128)S(1)} %reshape.36, s32[1024]{0:T(1024)S(1)} %pad_clamp_fusion), kind=kCustom, calls=%fused_computation | custom fusion | bytes 4194816 | tf_op jit(solution)/shard_map/jit(_take)/gather | solution.py:67
  167.6 0.0 copy-done
  167.6 3.4 %fusion.30 = bf16[128,4096]{1,0:T(8,128)(2,1)} fusion(bf16[128,4096]{1,0:T(8,128)(2,1)} %param.7, f32[128,4096]{1,0:T(8,128)} %gather_fusion, f32[128]{0:T(128)S(1)} %copy-done, pred[128]{0:T(512)(128)(4,1)S(1)} %get-tuple-element.5, pred[128]{0:T(512)(128)(4,1)S(1)} %get-tuple-element.8), kind=kLoop, calls=%fused_computation.23 | loop fusion | flops 3145728 | bytes 4195072 | tf_op jit(solution)/shard_map/convert_element_type | solution.py:69
  (2 shorter events, 0.0 us)
Async XLA Ops:
  49.9 3.2 %collective-permute-start = (bf16[16,20,2048]{2,0,1:T(8,128)(2,1)}, bf16[16,20,2048]{2,0,1:T(8,128)(2,1)S(1)}, u32[]{:S(2)}, u32[]{:S(2)}) collective-permute-start(bf16[16,20,2048]{2,0,1:T(8,128)(2,1)} %copy.15), channel_id=1, source_target_pairs={{0,1},{1,0},{2,3},{3,2},{4,5},{5,4},{6,7},{7,6},{8,9},{9,8},{10,11... | collective-permute-start | bytes 3932168 | tf_op jit(solution)/shard_map/ppermute | solution.py:11
  85.7 74.9 %all-to-all-start.1 = ((bf16[16,20,4096]{2,1,0:T(8,128)(2,1)}), bf16[16,20,4096]{2,1,0:T(8,128)(2,1)S(1)}, u32[]{:S(2)}, u32[]{:S(2)}) async-start(bf16[16,20,4096]{2,1,0:T(8,128)(2,1)} %reshape.35), calls=%async_computation.1 | async-start | bytes 6291456 | tf_op jit(solution)/shard_map/all_to_all | solution.py:60
  165.0 2.6 %copy-start = (f32[128]{0:T(128)S(1)}, f32[128]{0:T(128)}, u32[]{:S(2)}) copy-start(f32[128]{0:T(128)} %param.10) | copy-start | bytes 1540
where the time goes:
time: 171 us
  waiting for transfers between devices  71.7 us (42%)
  blocking collectives  42.4 us (25%)
  matrix products  30.1 us (18%)
  local copies, waits for them, and re-layouts  13.5 us (8%)
  other arithmetic  8 us (5%)
  starting transfers between devices  5.26 us (3%)
    all_to_all x1, waiting for transfers between devices, per_device(): lax.all_to_all(partial_value, 'expert', split_axis=0, concat_axis=0, tile...  69.9 us
    all_to_all x1, blocking collectives, per_device(): lax.all_to_all(sliced, 'expert', split_axis=0, concat_axis=0, tiled=True)  42.4 us
    dot_general x1, matrix products, per_device(): jnp.dot(hidden, weight_out, preferred_element_type=jnp.float32)  28.3 us
    all_to_all x1, starting transfers between devices, per_device(): lax.all_to_all(partial_value, 'expert', split_axis=0, concat_axis=0, tile...  5.05 us
    convert_element_type x1, other arithmetic, per_device(): return (widened + router_prob[:, None] * branch).astype(jnp.bfloat16)  3.43 us
  transfers between devices with their start and end apart: 2, of which 2 were waited for; matrix products, arithmetic and copies ran while one was open for 1% of the time, Pallas kernels for 0%

commit v1 on v0

--- a/solution.py
+++ b/solution.py
@@ -1,14 +1,340 @@
+import functools
+
 import jax
 import jax.numpy as jnp
+import numpy as np
 from jax import lax
+from jax.experimental import pallas as pl
+from jax.experimental.pallas import tpu as pltpu
 from jax.sharding import PartitionSpec as P
 
 EXP_WIN = 8
 CAP = 20
+Q = 4
+GROUP = 4
+SETS = ((2,), (3, 1, 0))
+TILE = 256
+MESH = pl.DeviceIdType.MESH
 
 
 def from_partner(x, axis, distance):
     return lax.ppermute(x, axis, [(i, i ^ 1 << distance) for i in range(lax.axis_size(axis))])
+
+
+def wait_bytes(ref, sem):
+    pltpu.make_async_copy(ref, ref, sem).wait()
+
+
+def kernel(
+    tok_ref, gain_ref, prob_ref, code_row_ref, code_col_ref, slot_col_ref, slot_row_ref, perm_ref, perm_t_ref,
+    win_hbm, wout_hbm, out_ref,
+    win, wout, placing, stacked, send_buf, recv_buf, x_buf, h_acc, hidden, pex_send, pex_recv, y_buf,
+    ret_send, ret_recv,
+    w_sem, send_sem, recv_sem, fwd_send_sem, fwd_recv_sem, pex_send_sem, pex_recv_sem, ret_send_sem, ret_recv_sem,
+):
+    n = 2 * EXP_WIN
+    rows, features = tok_ref.shape
+    half = features // 2
+    chunk = half // Q
+    block = Q * CAP
+    me = lax.axis_index("expert")
+    core = lax.rem(me, 2)
+    chip = me // 2
+    plane = me // GROUP
+    partner = me + 1 - 2 * core
+
+    barrier = pltpu.get_barrier_semaphore()
+
+    @pl.loop(1, n)
+    def _(i):
+        pl.semaphore_signal(barrier, inc=1, device_id={"expert": lax.rem(me + i, n)}, device_id_type=MESH)
+
+    own_col = pl.multiple_of(core * half, half)
+    other_col = pl.multiple_of((1 - core) * half, half)
+    loads = [
+        pltpu.make_async_copy(win_hbm.at[0, pl.ds(own_col, half), :], win.at[0], w_sem.at[0]),
+        pltpu.make_async_copy(win_hbm.at[0, pl.ds(other_col, half), :], win.at[1], w_sem.at[1]),
+        pltpu.make_async_copy(wout_hbm.at[0, :, pl.ds(other_col, half)], wout.at[0], w_sem.at[2]),
+        pltpu.make_async_copy(wout_hbm.at[0, :, pl.ds(own_col, half)], wout.at[1], w_sem.at[3]),
+    ]
+    for load in loads:
+        load.start()
+
+    @pl.loop(0, rows // 16)
+    def _(r):
+        top = pl.multiple_of(r * 16, 16)
+        widened = tok_ref[pl.ds(top, 16), :].astype(jnp.float32)
+        normed = (
+            widened
+            * lax.rsqrt(jnp.mean(widened * widened, axis=-1, keepdims=True) + 1e-06)
+            * gain_ref[...]
+        ).astype(jnp.bfloat16)
+        for h in range(2):
+            for q in range(Q):
+                at = h * half + q * chunk
+                stacked[h, pl.ds(pl.multiple_of(q * rows + top, 16), 16), :] = normed[:, at : at + chunk]
+
+    placing[...] = jnp.where(slot_col_ref[...] == code_row_ref[...], 1.0, 0.0).astype(jnp.bfloat16)
+    for h in range(2):
+        for t in range(chunk // TILE):
+            cols = slice(t * TILE, (t + 1) * TILE)
+            send_buf[h, :, cols] = jnp.dot(
+                placing[...], stacked[h, :, cols], preferred_element_type=jnp.float32
+            ).astype(jnp.bfloat16)
+
+    pl.semaphore_wait(barrier, n - 1)
+
+    for j in [g for s in SETS for g in s]:
+        for y in range(2):
+            dst_chip = jnp.bitwise_xor(plane, j) * 2 + y
+            src = [send_buf.at[h, pl.ds(pl.multiple_of(dst_chip * block, block), block), :] for h in range(2)]
+            spot = pl.multiple_of((j * GROUP + lax.rem(me, GROUP)) * block, block)
+            for h in range(2):
+                dst = dst_chip * 2 + h
+
+                def remote(src=src[h], dst=dst):
+                    pltpu.make_async_remote_copy(
+                        src_ref=src,
+                        dst_ref=recv_buf.at[pl.ds(spot, block), :],
+                        send_sem=send_sem,
+                        recv_sem=recv_sem.at[j],
+                        device_id={"expert": dst},
+                        device_id_type=MESH,
+                    ).start()
+
+                if j == 0:
+                    pl.when(dst != me)(remote)
+
+                    @pl.when(dst == me)
+                    def _(src=src[h]):
+                        pltpu.make_async_copy(
+                            src, recv_buf.at[pl.ds(spot, block), :], recv_sem.at[0]
+                        ).start()
+                else:
+                    remote()
+
+    offset = 0
+    for s, groups in enumerate(SETS):
+        m = len(groups) * GROUP * CAP
+        mine = pl.ds(offset, m)
+        for g, j in enumerate(groups):
+            seg = recv_buf.at[pl.ds(j * GROUP * block, GROUP * block), :]
+            wait_bytes(seg, recv_sem.at[j])
+            top = offset + g * GROUP * CAP
+            for t in range(chunk // TILE):
+                piece = jnp.dot(
+                    perm_ref[...], seg[:, t * TILE : (t + 1) * TILE], preferred_element_type=jnp.float32
+                ).astype(jnp.bfloat16)
+                for q in range(Q):
+                    x_buf[0, top : top + GROUP * CAP, q * chunk + t * TILE : q * chunk + (t + 1) * TILE] = piece[
+                        q * GROUP * CAP : (q + 1) * GROUP * CAP, :
+                    ]
+        forward = pltpu.make_async_remote_copy(
+            src_ref=x_buf.at[0, mine, :],
+            dst_ref=x_buf.at[1, mine, :],
+            send_sem=fwd_send_sem.at[s],
+            recv_sem=fwd_recv_sem.at[s],
+            device_id={"expert": partner},
+            device_id_type=MESH,
+        )
+        forward.start()
+        if s == 0:
+            loads[0].wait()
+
+        @pl.loop(0, hidden.shape[1] // TILE)
+        def _(t):
+            cols = pl.ds(pl.multiple_of(t * TILE, TILE), TILE)
+            h_acc[0:m, cols] = jnp.dot(x_buf[0, mine, :], win[0, :, cols], preferred_element_type=jnp.float32)
+
+        forward.wait_recv()
+        if s == 0:
+            loads[1].wait()
+
+        @pl.loop(0, hidden.shape[1] // TILE)
+        def _(t):
+            cols = pl.ds(pl.multiple_of(t * TILE, TILE), TILE)
+            total = h_acc[0:m, cols] + jnp.dot(
+                x_buf[1, mine, :], win[1, :, cols], preferred_element_type=jnp.float32
+            )
+            hidden[0:m, cols] = jnp.maximum(total, 0.0).astype(jnp.bfloat16)
+
+        if s == 0:
+            loads[2].wait()
+        exchange = []
+        for p in range(2):
+
+            @pl.loop(0, half // 2 // TILE)
+            def _(t):
+                cols = pl.ds(pl.multiple_of(p * (half // 2) + t * TILE, TILE), TILE)
+                to = pl.ds(pl.multiple_of(t * TILE, TILE), TILE)
+                pex_send[p, mine, to] = jnp.dot(
+                    hidden[0:m, :], wout[0, :, cols], preferred_element_type=jnp.float32
+                ).astype(jnp.bfloat16)
+
+            copy = pltpu.make_async_remote_copy(
+                src_ref=pex_send.at[p, mine, :],
+                dst_ref=pex_recv.at[p, mine, :],
+                send_sem=pex_send_sem.at[s, p],
+                recv_sem=pex_recv_sem.at[s, p],
+                device_id={"expert": partner},
+                device_id_type=MESH,
+            )
+            copy.start()
+            exchange.append(copy)
+        if s == 0:
+            loads[3].wait()
+        for p in range(2):
+            exchange[p].wait_recv()
+
+            @pl.loop(0, half // 2 // TILE)
+            def _(t):
+                cols = pl.ds(pl.multiple_of(p * (half // 2) + t * TILE, TILE), TILE)
+                to = pl.ds(pl.multiple_of(t * TILE, TILE), TILE)
+                y_buf[0:m, cols] = (
+                    jnp.dot(hidden[0:m, :], wout[1, :, cols], preferred_element_type=jnp.float32)
+                    + pex_recv[p, mine, to].astype(jnp.float32)
+                ).astype(jnp.bfloat16)
+
+        for g, j in enumerate(groups):
+            top = g * GROUP * CAP
+            base = j * GROUP * block
+            for t in range(chunk // TILE):
+                above = jnp.concatenate(
+                    [
+                        y_buf[top : top + GROUP * CAP, q * chunk + t * TILE : q * chunk + (t + 1) * TILE]
+                        for q in range(Q)
+                    ],
+                    axis=0,
+                )
+                ret_send[base : base + GROUP * block, t * TILE : (t + 1) * TILE] = jnp.dot(
+                    perm_t_ref[...], above, preferred_element_type=jnp.float32
+                ).astype(jnp.bfloat16)
+            for i in range(GROUP):
+                dst = jnp.bitwise_xor(plane, j) * GROUP + i
+                src = ret_send.at[pl.ds(base + i * block, block), :]
+                spot = ret_recv.at[core, pl.ds(pl.multiple_of(chip * block, block), block), :]
+
+                def remote(src=src, dst=dst, spot=spot):
+                    pltpu.make_async_remote_copy(
+                        src_ref=src,
+                        dst_ref=spot,
+                        send_sem=ret_send_sem,
+                        recv_sem=ret_recv_sem.at[core],
+                        device_id={"expert": dst},
+                        device_id_type=MESH,
+                    ).start()
+
+                if j == 0:
+                    pl.when(dst != me)(remote)
+
+                    @pl.when(dst == me)
+                    def _(src=src, spot=spot):
+                        pltpu.make_async_copy(src, spot, ret_recv_sem.at[core]).start()
+                else:
+                    remote()
+        offset += m
+
+    pick = stacked_pick(placing, code_col_ref, slot_row_ref)
+    for h in range(2):
+        wait_bytes(ret_recv.at[h], ret_recv_sem.at[h])
+        for q in range(Q):
+            for t in range(chunk // TILE):
+                at = h * half + q * chunk + t * TILE
+                picked = jnp.dot(
+                    pick[q], ret_recv[h, :, t * TILE : (t + 1) * TILE], preferred_element_type=jnp.float32
+                )
+                out_ref[:, at : at + TILE] = (
+                    tok_ref[:, at : at + TILE].astype(jnp.float32) + prob_ref[...] * picked
+                ).astype(jnp.bfloat16)
+
+    wait_bytes(recv_buf.at[pl.ds(0, (n - 1) * block), :], send_sem)
+    wait_bytes(recv_buf.at[pl.ds(0, (n - 1) * block), :], ret_send_sem)
+    offset = 0
+    for s, groups in enumerate(SETS):
+        m = len(groups) * GROUP * CAP
+        mine = pl.ds(offset, m)
+        wait_bytes(x_buf.at[0, mine, :], fwd_send_sem.at[s])
+        for p in range(2):
+            wait_bytes(pex_send.at[p, mine, :], pex_send_sem.at[s, p])
+        offset += m
+
+
+def stacked_pick(placing, code_col_ref, slot_row_ref):
+    rows = code_col_ref.shape[0] // Q
+    return [
+        jnp.where(code_col_ref[q * rows : (q + 1) * rows, :] == slot_row_ref[...], 1.0, 0.0).astype(jnp.bfloat16)
+        for q in range(Q)
+    ]
+
+
+def fused(tokens, routing, capacity_slot, router_prob, norm_gain, expert_in, expert_out):
+    rows, features = tokens.shape
+    half, chunk, block = features // 2, features // 2 // Q, Q * CAP
+    units = expert_in.shape[2]
+    slots = EXP_WIN * CAP
+    stride = 2 * slots
+    target = jnp.where(capacity_slot < CAP, routing * CAP + capacity_slot, -1)
+    code = (target[None, :] + (jnp.arange(Q, dtype=jnp.int32) * stride)[:, None]).reshape(Q * rows)
+    where = np.arange(EXP_WIN * block)
+    slot_code = (where % block // CAP * stride + where // block * CAP + where % CAP).astype(np.int32)
+    pos = np.arange(GROUP * block)
+    q, src, slot = pos // (GROUP * CAP), pos // CAP % GROUP, pos % CAP
+    perm = np.zeros((GROUP * block, GROUP * block), np.float32)
+    perm[pos, src * block + q * CAP + slot] = 1
+    largest = max(len(s) for s in SETS) * GROUP * CAP
+    total = 2 * EXP_WIN * CAP
+    vmem = pl.BlockSpec(memory_space=pltpu.VMEM)
+    hbm = pl.BlockSpec(memory_space=pl.ANY)
+    bf16 = jnp.bfloat16
+    return pl.pallas_call(
+        kernel,
+        out_shape=jax.ShapeDtypeStruct(tokens.shape, tokens.dtype),
+        in_specs=[vmem] * 9 + [hbm] * 2,
+        out_specs=vmem,
+        scratch_shapes=[
+            pltpu.VMEM((2, half, units), bf16),
+            pltpu.VMEM((2, units, half), bf16),
+            pltpu.VMEM((EXP_WIN * block, Q * rows), bf16),
+            pltpu.VMEM((2, Q * rows, chunk), bf16),
+            pltpu.VMEM((2, EXP_WIN * block, chunk), bf16),
+            pltpu.VMEM((2 * EXP_WIN * block, chunk), bf16),
+            pltpu.VMEM((2, total, half), bf16),
+            pltpu.VMEM((largest, units), jnp.float32),
+            pltpu.VMEM((largest, units), bf16),
+            pltpu.VMEM((2, total, half // 2), bf16),
+            pltpu.VMEM((2, total, half // 2), bf16),
+            pltpu.VMEM((largest, half), bf16),
+            pltpu.VMEM((2 * EXP_WIN * block, chunk), bf16),
+            pltpu.VMEM((2, EXP_WIN * block, chunk), bf16),
+            pltpu.SemaphoreType.DMA((4,)),
+            pltpu.SemaphoreType.DMA,
+            pltpu.SemaphoreType.DMA((GROUP,)),
+            pltpu.SemaphoreType.DMA((len(SETS),)),
+            pltpu.SemaphoreType.DMA((len(SETS),)),
+            pltpu.SemaphoreType.DMA((len(SETS), 2)),
+            pltpu.SemaphoreType.DMA((len(SETS), 2)),
+            pltpu.SemaphoreType.DMA,
+            pltpu.SemaphoreType.DMA((2,)),
+        ],
+        compiler_params=pltpu.CompilerParams(
+            collective_id=0, has_side_effects=True, vmem_limit_bytes=63 * 1024 * 1024
+        ),
+        cost_estimate=pl.CostEstimate(
+            flops=4 * total * features * units, bytes_accessed=4 * features * units, transcendentals=0
+        ),
+    )(
+        tokens,
+        norm_gain[None, :],
+        router_prob[:, None],
+        code[None, :],
+        code[:, None],
+        jnp.asarray(slot_code[:, None]),
+        jnp.asarray(slot_code[None, :]),
+        jnp.asarray(perm, bf16),
+        jnp.asarray(perm.T, bf16),
+        expert_in,
+        expert_out,
+    )
 
 
 def per_device(tokens, routing, capacity_slot, router_prob, norm_gain, expert_in, expert_out):
@@ -79,8 +405,9 @@
         P("expert", None, None),
         P("expert", None, None),
     )
+    two_holders = mesh.shape["expert"] == 2 * EXP_WIN
     return jax.shard_map(
-        per_device,
+        fused if two_holders else per_device,
         mesh=mesh,
         in_specs=placed,
         out_specs=P(("groups", "expert"), None),

time: 171 us -> 83.5 us (0.49)
  Pallas kernels: 0 us -> 77.9 us
  waiting for transfers between devices: 71.7 us -> 0 us
  blocking collectives: 42.4 us -> 0 us
  matrix products: 30.1 us -> 0 us
  local copies, waits for them, and re-layouts: 13.5 us -> 4.54 us
  other arithmetic: 8 us -> 0.75 us
  starting transfers between devices: 5.26 us -> 0 us
    pallas_call x0 -> x1, Pallas kernels: none -> 77.9 us  [fused(): pl.pallas_call(kernel, out_shape=jax.ShapeDtypeStruct(tokens.shape, token...]
    all_to_all x1 -> x0, waiting for transfers between devices: 69.9 us -> none  [per_device(): lax.all_to_all(partial_value, 'expert', split_axis=0, concat_axis=0, tile...]
    all_to_all x1 -> x0, blocking collectives: 42.4 us -> none  [per_device(): lax.all_to_all(sliced, 'expert', split_axis=0, concat_axis=0, tiled=True)]
    dot_general x2 -> x0, matrix products: 30.1 us -> none  [the longest x1 28.3 us: per_device(): jnp.dot(hidden, weight_out, preferred_element_type=jnp.float32)]
    all_to_all x1 -> x0, starting transfers between devices: 5.05 us -> none  [per_device(): lax.all_to_all(partial_value, 'expert', split_axis=0, concat_axis=0, tile...]
    reshape x3 -> x0, local copies, waits for them, and re-layouts: 4.97 us -> none  [the longest x1 2.35 us: per_device(): partial_value = partial_value.reshape(devices, slot_count, features)]
    reduce_sum x2 -> x0, other arithmetic: 3.86 us -> none  [the longest x1 2.35 us: per_device(): combined = returned.reshape(EXP_WIN, holders, CAP, features).astype(jnp.f...]
    convert_element_type x1 -> x0, other arithmetic: 3.43 us -> none  [per_device(): return (widened + router_prob[:, None] * branch).astype(jnp.bfloat16)]
  transfers between devices with their start and end apart: 2 -> 0, of which waited for: 2 -> 0; matrix products, arithmetic and copies ran while one was open for 1% -> 0% of each run, Pallas kernels for 0% -> 0%
where the time goes in v1:
time: 83.5 us; the launch traced here: 83.3 us
  Pallas kernels  77.9 us (93%)
  local copies, waits for them, and re-layouts  4.54 us (5%)
    pallas_call x1, Pallas kernels, fused(): pl.pallas_call(kernel, out_shape=jax.ShapeDtypeStruct(tokens.shape, token...  77.9 us
    unnamed x3, local copies, waits for them, and re-layouts  2.29 us

profile of v1, /device:TPU:15, one launch (start us, length us, event | category | flops | bytes accessed | tf_op | source)
XLA Modules:
  0.0 83.3 jit_solution(4239033404718231838)
XLA Ops:
  0.0 0.7 compare_select_fusion
  0.7 0.1 broadcast_add_fusion
  0.8 0.0 copy-start
  0.8 1.4 %copy.13.prob_ref = f32[128,1]{1,0:T(8,128)} copy(f32[128,1]{0,1:T(1,128)} %bitcast.6) | data formatting | bytes 1024 | tf_op jit(solution)/shard_map/broadcast_in_dim | solution.py:328
  2.1 0.9 %copy.14.code_col_ref = s32[512,1]{1,0:T(8,128)} copy(s32[512,1]{0,1:T(1,128)S(1)} %bitcast.4) | data formatting | bytes 4096 | tf_op jit(solution)/shard_map/add | solution.py:277
  3.0 0.0 copy-done
  3.0 77.9 %shard_map.109 = bf16[128,4096]{1,0:T(8,128)(2,1)} custom-call(bf16[128,4096]{1,0:T(8,128)(2,1)} %tok_ref.1, f32[1,4096]{1,0:T(1,128)} %bitcast.7, f32[128,1]{1,0:T(8,128)} %copy.13.prob_ref, s32[1,512]{1,0:T(1,128)} %bitcast.5, s32[512,1]{1,0:T(8,128)} %copy.14.code_col_ref, s32[640,1]{1,0:T(8,128)} %constant.12.clone.slot_col_ref, ...), custom_call_target="tpu_custom_call" | custom-call | flops 13421772800 | bytes 41943040 | tf_op jit(solution)/shard_map/pallas_call | solution.py:289
  81.0 2.3 %copy.16 = bf16[128,4096]{1,0:T(8,128)(2,1)} copy(bf16[128,4096]{1,0:T(8,128)(2,1)} %shard_map.109) | data formatting | bytes 2097152
  (1 shorter events, 0.0 us)
Async XLA Ops:
  0.8 2.3 %copy-start = (s32[4,128]{1,0:T(4,128)}, s32[4,128]{1,0:T(4,128)S(1)}, u32[]{:S(2)}) copy-start(s32[4,128]{1,0:T(4,128)S(1)} %broadcast_add_fusion) | copy-start | bytes 6148

commit v2 on v1

--- a/solution.py
+++ b/solution.py
@@ -12,7 +12,8 @@
 CAP = 20
 Q = 4
 GROUP = 4
-SETS = ((2,), (3, 1, 0))
+SETS = ((2,1),(3,0))
+ORDER = ((2, 0), (1, 0), (2, 1), (1, 1), (3, 0), (0, 0), (3, 1), (0, 1))
 TILE = 256
 MESH = pl.DeviceIdType.MESH
 
@@ -26,7 +27,7 @@
 
 
 def kernel(
-    tok_ref, gain_ref, prob_ref, code_row_ref, code_col_ref, slot_col_ref, slot_row_ref, perm_ref, perm_t_ref,
+    tok_ref, gain_ref, routing_ref, capacity_ref, slot_col_ref, slot_row_ref, perm_ref, perm_t_ref,
     win_hbm, wout_hbm, out_ref,
     win, wout, placing, stacked, send_buf, recv_buf, x_buf, h_acc, hidden, pex_send, pex_recv, y_buf,
     ret_send, ret_recv,
@@ -74,7 +75,13 @@
                 at = h * half + q * chunk
                 stacked[h, pl.ds(pl.multiple_of(q * rows + top, 16), 16), :] = normed[:, at : at + chunk]
 
-    placing[...] = jnp.where(slot_col_ref[...] == code_row_ref[...], 1.0, 0.0).astype(jnp.bfloat16)
+    kept = capacity_ref[...] < CAP
+    target = jnp.where(kept, routing_ref[...] * CAP + capacity_ref[...], -1)
+    stride = 2 * EXP_WIN * CAP
+    for q in range(Q):
+        placing[:, q * rows : (q + 1) * rows] = jnp.where(
+            slot_col_ref[...] == target + q * stride, 1.0, 0.0
+        ).astype(jnp.bfloat16)
     for h in range(2):
         for t in range(chunk // TILE):
             cols = slice(t * TILE, (t + 1) * TILE)
@@ -84,34 +91,33 @@
 
     pl.semaphore_wait(barrier, n - 1)
 
-    for j in [g for s in SETS for g in s]:
-        for y in range(2):
-            dst_chip = jnp.bitwise_xor(plane, j) * 2 + y
-            src = [send_buf.at[h, pl.ds(pl.multiple_of(dst_chip * block, block), block), :] for h in range(2)]
-            spot = pl.multiple_of((j * GROUP + lax.rem(me, GROUP)) * block, block)
-            for h in range(2):
-                dst = dst_chip * 2 + h
-
-                def remote(src=src[h], dst=dst):
-                    pltpu.make_async_remote_copy(
-                        src_ref=src,
-                        dst_ref=recv_buf.at[pl.ds(spot, block), :],
-                        send_sem=send_sem,
-                        recv_sem=recv_sem.at[j],
-                        device_id={"expert": dst},
-                        device_id_type=MESH,
+    for j, y in ORDER:
+        dst_chip = jnp.bitwise_xor(plane, j) * 2 + y
+        src = [send_buf.at[h, pl.ds(pl.multiple_of(dst_chip * block, block), block), :] for h in range(2)]
+        spot = pl.multiple_of((j * GROUP + lax.rem(me, GROUP)) * block, block)
+        for h in range(2):
+            dst = dst_chip * 2 + h
+
+            def remote(src=src[h], dst=dst):
+                pltpu.make_async_remote_copy(
+                    src_ref=src,
+                    dst_ref=recv_buf.at[pl.ds(spot, block), :],
+                    send_sem=send_sem,
+                    recv_sem=recv_sem.at[j],
+                    device_id={"expert": dst},
+                    device_id_type=MESH,
+                ).start()
+
+            if j == 0:
+                pl.when(dst != me)(remote)
+
+                @pl.when(dst == me)
+                def _(src=src[h]):
+                    pltpu.make_async_copy(
+                        src, recv_buf.at[pl.ds(spot, block), :], recv_sem.at[0]
                     ).start()
-
-                if j == 0:
-                    pl.when(dst != me)(remote)
-
-                    @pl.when(dst == me)
-                    def _(src=src[h]):
-                        pltpu.make_async_copy(
-                            src, recv_buf.at[pl.ds(spot, block), :], recv_sem.at[0]
-                        ).start()
-                else:
-                    remote()
+            else:
+                remote()
 
     offset = 0
     for s, groups in enumerate(SETS):
@@ -209,7 +215,9 @@
                 ret_send[base : base + GROUP * block, t * TILE : (t + 1) * TILE] = jnp.dot(
                     perm_t_ref[...], above, preferred_element_type=jnp.float32
                 ).astype(jnp.bfloat16)
-            for i in range(GROUP):
+        for i in range(GROUP):
+            for j in groups:
+                base = j * GROUP * block
                 dst = jnp.bitwise_xor(plane, j) * GROUP + i
                 src = ret_send.at[pl.ds(base + i * block, block), :]
                 spot = ret_recv.at[core, pl.ds(pl.multiple_of(chip * block, block), block), :]
@@ -234,17 +242,18 @@
                     remote()
         offset += m
 
-    pick = stacked_pick(placing, code_col_ref, slot_row_ref)
+    diagonal = lax.broadcasted_iota(jnp.int32, (rows, rows), 0) == lax.broadcasted_iota(jnp.int32, (rows, rows), 1)
+    target_col = jnp.sum(jnp.where(diagonal, target, 0), axis=1, keepdims=True)
+    pick = [
+        jnp.where(target_col + q * stride == slot_row_ref[...], 1.0, 0.0).astype(jnp.bfloat16) for q in range(Q)
+    ]
     for h in range(2):
         wait_bytes(ret_recv.at[h], ret_recv_sem.at[h])
         for q in range(Q):
             for t in range(chunk // TILE):
                 at = h * half + q * chunk + t * TILE
-                picked = jnp.dot(
+                out_ref[:, at : at + TILE] = jnp.dot(
                     pick[q], ret_recv[h, :, t * TILE : (t + 1) * TILE], preferred_element_type=jnp.float32
-                )
-                out_ref[:, at : at + TILE] = (
-                    tok_ref[:, at : at + TILE].astype(jnp.float32) + prob_ref[...] * picked
                 ).astype(jnp.bfloat16)
 
     wait_bytes(recv_buf.at[pl.ds(0, (n - 1) * block), :], send_sem)
@@ -259,22 +268,12 @@
         offset += m
 
 
-def stacked_pick(placing, code_col_ref, slot_row_ref):
-    rows = code_col_ref.shape[0] // Q
-    return [
-        jnp.where(code_col_ref[q * rows : (q + 1) * rows, :] == slot_row_ref[...], 1.0, 0.0).astype(jnp.bfloat16)
-        for q in range(Q)
-    ]
-
-
 def fused(tokens, routing, capacity_slot, router_prob, norm_gain, expert_in, expert_out):
     rows, features = tokens.shape
     half, chunk, block = features // 2, features // 2 // Q, Q * CAP
     units = expert_in.shape[2]
     slots = EXP_WIN * CAP
     stride = 2 * slots
-    target = jnp.where(capacity_slot < CAP, routing * CAP + capacity_slot, -1)
-    code = (target[None, :] + (jnp.arange(Q, dtype=jnp.int32) * stride)[:, None]).reshape(Q * rows)
     where = np.arange(EXP_WIN * block)
     slot_code = (where % block // CAP * stride + where // block * CAP + where % CAP).astype(np.int32)
     pos = np.arange(GROUP * block)
@@ -286,10 +285,10 @@
     vmem = pl.BlockSpec(memory_space=pltpu.VMEM)
     hbm = pl.BlockSpec(memory_space=pl.ANY)
     bf16 = jnp.bfloat16
-    return pl.pallas_call(
+    branch = pl.pallas_call(
         kernel,
         out_shape=jax.ShapeDtypeStruct(tokens.shape, tokens.dtype),
-        in_specs=[vmem] * 9 + [hbm] * 2,
+        in_specs=[vmem] * 8 + [hbm] * 2,
         out_specs=vmem,
         scratch_shapes=[
             pltpu.VMEM((2, half, units), bf16),
@@ -325,9 +324,8 @@
     )(
         tokens,
         norm_gain[None, :],
-        router_prob[:, None],
-        code[None, :],
-        code[:, None],
+        routing[None, :],
+        capacity_slot[None, :],
         jnp.asarray(slot_code[:, None]),
         jnp.asarray(slot_code[None, :]),
         jnp.asarray(perm, bf16),
@@ -335,6 +333,7 @@
         expert_in,
         expert_out,
     )
+    return (tokens.astype(jnp.float32) + router_prob[:, None] * branch.astype(jnp.float32)).astype(jnp.bfloat16)
 
 
 def per_device(tokens, routing, capacity_slot, router_prob, norm_gain, expert_in, expert_out):

time: 83.5 us -> 73.7 us (0.88)
  Pallas kernels: 77.9 us -> 70.6 us
  local copies, waits for them, and re-layouts: 4.54 us -> 0.01 us
  other arithmetic: 0.75 us -> 2.93 us
    pallas_call x1, Pallas kernels: 77.9 us -> 70.6 us  [fused(): pl.pallas_call(kernel, out_shape=jax.ShapeDtypeStruct(tokens.shape, token...]
    convert_element_type x0 -> x1, other arithmetic: none -> 2.93 us  [fused(): (tokens.astype(jnp.float32) + router_prob[:, None] * branch.astype(jnp.fl...]
    unnamed x3 -> x2, local copies, waits for them, and re-layouts: 2.29 us -> 0.01 us
    broadcast_in_dim x1 -> x0, local copies, waits for them, and re-layouts: 1.39 us -> none  [fused(): router_prob[:, None]]
    add x1 -> x0, local copies, waits for them, and re-layouts: 0.86 us -> none  [fused(): target[None, :] + (jnp.arange(Q, dtype=jnp.int32) * stride)[:, None]]
where the time goes in v2:
time: 73.7 us; the launch traced here: 73.6 us
  Pallas kernels  70.6 us (96%)
  other arithmetic  2.93 us (4%)
    pallas_call x1, Pallas kernels, fused(): pl.pallas_call(kernel, out_shape=jax.ShapeDtypeStruct(tokens.shape, token...  70.6 us
    convert_element_type x1, other arithmetic, fused(): (tokens.astype(jnp.float32) + router_prob[:, None] * branch.astype(jnp.fl...  2.93 us

profile of v2, /device:TPU:15, one launch (start us, length us, event | category | flops | bytes accessed | tf_op | source)
XLA Modules:
  0.0 73.6 jit_solution(14012697995643570875)
XLA Ops:
  0.0 0.0 copy-start
  0.0 70.6 %shard_map.109 = bf16[128,4096]{1,0:T(8,128)(2,1)} custom-call(bf16[128,4096]{1,0:T(8,128)(2,1)} %tok_ref.1, f32[1,4096]{1,0:T(1,128)} %bitcast.3, s32[1,128]{1,0:T(1,128)} %bitcast.4, s32[1,128]{1,0:T(1,128)} %bitcast.5, s32[640,1]{1,0:T(8,128)} %constant.6.clone.slot_col_ref, s32[1,640]{1,0:T(1,128)} %constant.7.clone.slot_row_ref, ...), custom_call_target="tpu_custom_call" | custom-call | flops 13421772800 | bytes 41943040 | tf_op jit(solution)/shard_map/pallas_call | solution.py:288
  70.6 0.0 copy-done
  70.6 2.9 %add_convert_fusion = bf16[128,4096]{1,0:T(8,128)(2,1)} fusion(bf16[128,4096]{1,0:T(8,128)(2,1)} %shard_map.109, bf16[128,4096]{1,0:T(8,128)(2,1)} %tok_ref.1, f32[128]{0:T(128)S(1)} %copy-done), kind=kLoop, calls=%fused_computation | loop fusion | flops 2621440 | bytes 3146240 | tf_op jit(solution)/shard_map/convert_element_type | solution.py:336
Async XLA Ops:
  0.0 70.6 %copy-start = (f32[128]{0:T(128)S(1)}, f32[128]{0:T(128)}, u32[]{:S(2)}) copy-start(f32[128]{0:T(128)} %param.14) | copy-start | bytes 1540

commit v3 on v2

--- a/solution.py
+++ b/solution.py
@@ -13,7 +13,7 @@
 Q = 4
 GROUP = 4
 SETS = ((2,1),(3,0))
-ORDER = ((2, 0), (1, 0), (2, 1), (1, 1), (3, 0), (0, 0), (3, 1), (0, 1))
+ORDER = ((2, 0), (2, 1), (1, 0), (1, 1), (3, 0), (3, 1), (0, 0), (0, 1))
 TILE = 256
 MESH = pl.DeviceIdType.MESH
 
@@ -82,17 +82,16 @@
         placing[:, q * rows : (q + 1) * rows] = jnp.where(
             slot_col_ref[...] == target + q * stride, 1.0, 0.0
         ).astype(jnp.bfloat16)
-    for h in range(2):
-        for t in range(chunk // TILE):
-            cols = slice(t * TILE, (t + 1) * TILE)
-            send_buf[h, :, cols] = jnp.dot(
-                placing[...], stacked[h, :, cols], preferred_element_type=jnp.float32
-            ).astype(jnp.bfloat16)
-
     pl.semaphore_wait(barrier, n - 1)
 
     for j, y in ORDER:
-        dst_chip = jnp.bitwise_xor(plane, j) * 2 + y
+        if y == 0:
+            bound = pl.ds(pl.multiple_of(jnp.bitwise_xor(plane, j) * 2 * block, 2 * block), 2 * block)
+            for h in range(2):
+                send_buf[h, bound, :] = jnp.dot(
+                    placing[bound, :], stacked[h], preferred_element_type=jnp.float32
+                ).astype(jnp.bfloat16)
+        dst_chip = jnp.bitwise_xor(chip, j * 2 + y)
         src = [send_buf.at[h, pl.ds(pl.multiple_of(dst_chip * block, block), block), :] for h in range(2)]
         spot = pl.multiple_of((j * GROUP + lax.rem(me, GROUP)) * block, block)
         for h in range(2):
@@ -108,7 +107,7 @@
                     device_id_type=MESH,
                 ).start()
 
-            if j == 0:
+            if j == 0 and y == 0:
                 pl.when(dst != me)(remote)
 
                 @pl.when(dst == me)
@@ -215,11 +214,10 @@
                 ret_send[base : base + GROUP * block, t * TILE : (t + 1) * TILE] = jnp.dot(
                     perm_t_ref[...], above, preferred_element_type=jnp.float32
                 ).astype(jnp.bfloat16)
-        for i in range(GROUP):
+        for i in (0, 2, 1, 3):
             for j in groups:
-                base = j * GROUP * block
-                dst = jnp.bitwise_xor(plane, j) * GROUP + i
-                src = ret_send.at[pl.ds(base + i * block, block), :]
+                dst = jnp.bitwise_xor(me, j * GROUP + i)
+                src = ret_send.at[pl.ds(pl.multiple_of((j * GROUP + lax.rem(dst, GROUP)) * block, block), block), :]
                 spot = ret_recv.at[core, pl.ds(pl.multiple_of(chip * block, block), block), :]
 
                 def remote(src=src, dst=dst, spot=spot):
@@ -232,12 +230,8 @@
                         device_id_type=MESH,
                     ).start()
 
-                if j == 0:
-                    pl.when(dst != me)(remote)
-
-                    @pl.when(dst == me)
-                    def _(src=src, spot=spot):
-                        pltpu.make_async_copy(src, spot, ret_recv_sem.at[core]).start()
+                if j == 0 and i == 0:
+                    pltpu.make_async_copy(src, spot, ret_recv_sem.at[core]).start()
                 else:
                     remote()
         offset += m

time: 73.7 us -> 76.5 us (1.038)
  the two profiles are of different devices: /device:TPU:15 before, /device:TPU:17 now
where the time goes in v3:
time: 76.5 us; the launch traced here: 76.4 us
  Pallas kernels  73.4 us (96%)
  other arithmetic  2.93 us (4%)
    pallas_call x1, Pallas kernels, fused(): pl.pallas_call(kernel, out_shape=jax.ShapeDtypeStruct(tokens.shape, token...  73.4 us
    convert_element_type x1, other arithmetic, fused(): (tokens.astype(jnp.float32) + router_prob[:, None] * branch.astype(jnp.fl...  2.93 us

profile of v3, /device:TPU:17, one launch (start us, length us, event | category | flops | bytes accessed | tf_op | source)
XLA Modules:
  0.0 76.4 jit_solution(1311995087939036578)
XLA Ops:
  0.0 0.0 copy-start
  0.0 73.4 %shard_map.109 = bf16[128,4096]{1,0:T(8,128)(2,1)} custom-call(bf16[128,4096]{1,0:T(8,128)(2,1)} %tok_ref.1, f32[1,4096]{1,0:T(1,128)} %bitcast.3, s32[1,128]{1,0:T(1,128)} %bitcast.4, s32[1,128]{1,0:T(1,128)} %bitcast.5, s32[640,1]{1,0:T(8,128)} %constant.6.clone.slot_col_ref, s32[1,640]{1,0:T(1,128)} %constant.7.clone.slot_row_ref, ...), custom_call_target="tpu_custom_call" | custom-call | flops 13421772800 | bytes 41943040 | tf_op jit(solution)/shard_map/pallas_call | solution.py:282
  73.4 0.0 copy-done
  73.4 2.9 %add_convert_fusion = bf16[128,4096]{1,0:T(8,128)(2,1)} fusion(bf16[128,4096]{1,0:T(8,128)(2,1)} %shard_map.109, bf16[128,4096]{1,0:T(8,128)(2,1)} %tok_ref.1, f32[128]{0:T(128)S(1)} %copy-done), kind=kLoop, calls=%fused_computation | loop fusion | flops 2621440 | bytes 3146240 | tf_op jit(solution)/shard_map/convert_element_type | solution.py:330
Async XLA Ops:
  0.0 73.4 %copy-start = (f32[128]{0:T(128)S(1)}, f32[128]{0:T(128)}, u32[]{:S(2)}) copy-start(f32[128]{0:T(128)} %param.14) | copy-start | bytes 1540
